TPU v7x, 512 devices: a whole 4x8x8 slice. The times are simulated.
512 devices in a mesh: gx: 8 (over y), gy: 8 (over x, core), gz: 8 (over z).
Axes of the slice: x: 4, y: 8, z: 8, core: 2. Of those that a mesh axis runs over, the one named last changes fastest.
Arguments:
- positions: float32 [2, 48, 1024, 1024], P(None, 'gz', 'gy', 'gx'), may hold values from -1.2 to 1.2
- velocities: float32 [2, 48, 1024, 1024], P(None, 'gz', 'gy', 'gx'), may hold values from -18 to 18, as said below
- link_codes: int32 [48, 1024, 1024], P('gz', 'gy', 'gx'), may hold values from 0 to 4095, as said below
- fixed_nodes: int32 [48, 1024, 1024], P('gz', 'gy', 'gx'), may hold values 0 or 1
Outputs:
- final_positions: float32 [2, 48, 1024, 1024], P(None, 'gz', 'gy', 'gx')
- final_velocities: float32 [2, 48, 1024, 1024], P(None, 'gz', 'gy', 'gx')
Inputs may be any that keep to these rules, and one draw needn't show every extreme that they name: `link_codes`: bit b of an entry is set exactly when the node's link b is valid; a link and its reverse link at the neighbour agree, and links that leave the grid are never set. velocities are finite.
All inputs are finite; a program needn't handle non-finite values. No bound on the sum of `fixed_nodes` on one device may be relied on, other than what follows from the above.
Results may differ from a plain program's by a relative error of at most 0.0001.
Values sent between devices are 32-bit elements; how exact they have to be, the bound alone decides.
A program may use at most 64 MiB of HBM per device.

v0:
```python
import math

import jax
import jax.numpy as jnp
from jax import lax
from jax.sharding import PartitionSpec as P

ITERS = 3


PLANE_LINKS = [(0, 1), (0, -1), (1, 0), (-1, 0), (1, 1), (-1, -1), (1, -1), (-1, 1)]
DEPTH_LINKS = [(1, 0.5), (-1, 0.5), (2, 0.25), (-2, 0.25)]
TIME_STEP = 0.3
DAMPING = 0.9
STIFF_PLANE = 1.0
HUBER_DELTA = 0.5
LENGTH_FLOOR = 0.25
ENERGY_CAP = 0.04
EPSILON = 1e-06


def extended(block, sides, width):
    for axis, dim in sides:
        count = lax.axis_size(axis)
        forward = [(i, i + 1) for i in range(count - 1)]
        backward = [(target, source) for source, target in forward]
        low = lax.ppermute(
            lax.slice_in_dim(block, block.shape[dim] - width, None, axis=dim), axis, forward
        )
        high = lax.ppermute(lax.slice_in_dim(block, 0, width, axis=dim), axis, backward)
        block = jnp.concatenate([low, block, high], axis=dim)
    return block


def spring_force(center, plane_ext, depth_ext, links):
    depth, rows, cols = (center.shape[1], center.shape[2], center.shape[3])
    force_y = jnp.zeros(center.shape[1:], jnp.float32)
    force_x = jnp.zeros(center.shape[1:], jnp.float32)
    for bit_index, (off_y, off_x) in enumerate(PLANE_LINKS):
        neighbour = plane_ext[:, :, 1 + off_y : 1 + off_y + rows, 1 + off_x : 1 + off_x + cols]
        delta_y = off_y + neighbour[0] - center[0]
        delta_x = off_x + neighbour[1] - center[1]
        length = jnp.sqrt(delta_y * delta_y + delta_x * delta_x)
        rest_len = math.sqrt(off_y * off_y + off_x * off_x)
        active = (links >> bit_index & 1).astype(jnp.float32)
        magnitude = (
            active
            * STIFF_PLANE
            * jnp.clip(length - rest_len, -HUBER_DELTA, HUBER_DELTA)
            / jnp.maximum(length, LENGTH_FLOOR)
        )
        force_y = force_y + magnitude * delta_y
        force_x = force_x + magnitude * delta_x
    for link_index, (off_z, stiffness) in enumerate(DEPTH_LINKS):
        neighbour = depth_ext[:, 2 + off_z : 2 + off_z + depth]
        delta_y = neighbour[0] - center[0]
        delta_x = neighbour[1] - center[1]
        length = jnp.sqrt(delta_y * delta_y + delta_x * delta_x)
        active = (links >> 8 + link_index & 1).astype(jnp.float32)
        magnitude = active * stiffness * HUBER_DELTA / jnp.maximum(length, HUBER_DELTA)
        force_y = force_y + magnitude * delta_y
        force_x = force_x + magnitude * delta_x
    return jnp.stack([force_y, force_x])


def extend_field(field):
    plane_ext = extended(field, (("gx", 3), ("gy", 2)), 1)
    depth_ext = extended(field, (("gz", 1),), 2)
    return (plane_ext, depth_ext)


def total_energy(kicked):
    return lax.psum(0.5 * jnp.sum(kicked * kicked), ("gx", "gy", "gz"))


def local(positions, velocities, link_codes, fixed_nodes):
    movable = (1 - fixed_nodes).astype(jnp.float32)
    nodes_all = (
        positions.shape[1]
        * positions.shape[2]
        * positions.shape[3]
        * lax.axis_size("gx")
        * lax.axis_size("gy")
        * lax.axis_size("gz")
    )
    capacity = ENERGY_CAP * nodes_all
    position = positions
    velocity = velocities
    for iteration in range(ITERS):
        plane_ext, depth_ext = extend_field(position)
        force = spring_force(position, plane_ext, depth_ext, link_codes)
        kicked = (DAMPING * velocity + TIME_STEP * force) * movable
        kinetic = total_energy(kicked)
        factor = jnp.minimum(1.0, jnp.sqrt(capacity / (kinetic + EPSILON)))
        velocity = factor * kicked
        position = position + TIME_STEP * velocity
    return (position, velocity)


def solution(mesh):
    in_specs = (
        P(None, "gz", "gy", "gx"),
        P(None, "gz", "gy", "gx"),
        P("gz", "gy", "gx"),
        P("gz", "gy", "gx"),
    )
    out_specs = (P(None, "gz", "gy", "gx"), P(None, "gz", "gy", "gx"))
    return jax.shard_map(local, mesh=mesh, in_specs=in_specs, out_specs=out_specs, check_vma=False)
```

profile of v0, /device:TPU:1, one launch (start us, length us, event | category | flops | bytes accessed | tf_op | source)
XLA Modules:
  0.0 405.7 jit_solution(3673762710779870098)
XLA Ops:
  0.6 1.9 fusion.170
  4.3 4.7 %collective-permute-start.1 = (f32[2,6,128,1]{2,0,3,1:T(2,128)S(1)}, f32[2,6,128,1]{2,0,3,1:T(2,128)S(1)}, u32[]{:S(2)}, u32[]{:S(2)}) collective-permute-start(f32[2,6,128,1]{2,0,3,1:T(2,128)S(1)} %copy.139), channel_id=1, source_target_pairs={{0,64},{64,128},{128,192},{192,256},{256,320},{320,384},{384,448},... | collective-permute-start | bytes 18440 | tf_op jit(solution)/shard_map/ppermute | solution.py:27
  9.8 4.8 %collective-permute-start.5 = (f32[2,2,128,128]{3,2,1,0:T(8,128)}, f32[2,2,128,128]{3,2,1,0:T(8,128)}, u32[]{:S(2)}, u32[]{:S(2)}) collective-permute-start(f32[2,2,128,128]{3,2,1,0:T(8,128)} %get-tuple-element.53), channel_id=1, source_target_pairs={{0,1},{1,2},{2,3},{3,4},{4,5},{5,6},{6,7},{8,9},{9,10},{10,11},{11... | collective-permute-start | bytes 786440 | tf_op jit(solution)/shard_map/ppermute | solution.py:27
  16.8 5.8 %collective-permute-start.2 = (f32[2,6,1,130]{3,0,2,1:T(2,128)S(1)}, f32[2,6,1,130]{3,0,2,1:T(2,128)S(1)}, u32[]{:S(2)}, u32[]{:S(2)}) collective-permute-start(f32[2,6,1,130]{3,0,2,1:T(2,128)S(1)} %copy.114), channel_id=1, source_target_pairs={{8,0},{16,8},{24,16},{32,24},{40,32},{48,40},{56,48},{9,1},{17,9},... | collective-permute-start | bytes 18728 | tf_op jit(solution)/shard_map/ppermute | solution.py:30
  22.6 1.9 collective-permute-start.3
  28.3 4.1 %add_bitcast_fusion.5 = (f32[1,6,128,128]{3,2,1,0:T(8,128)S(1)}, f32[6,128,128]{2,1,0:T(8,128)S(1)}, f32[6,128,128]{2,1,0:T(8,128)S(1)}, f32[6,128,128]{2,1,0:T(8,128)S(1)}, f32[6,128,128]{2,1,0:T(8,128)S(1)}) fusion(f32[2,8,128,128]{3,2,1,0:T(8,128)S(1)} %constant_dynamic-update-slice_fusion, f32[2,8,128,128]{3,2,1,0:T(8,128)S(1)} %get-tuple-element.51, ...), kind=kLoop, calls=%fused_computation.278 | loop fusion | flops 18382848 | bytes 13369344 | tf_op jit(solution)/shard_map/stack | solution.py:63
  32.4 3.8 add_bitcast_fusion.4
  37.7 102.5 %psum.21 = f32[]{:T(128)} all-reduce(f32[]{:T(128)S(6)} %mul.687), channel_id=1, replica_groups=mesh['gx'=8,'gy'=8,'gz'=8] {'gx','gy','gz'}, use_global_device_ids=true, to_apply=%region_1.2 | all-reduce | flops 1 | bytes 8 | tf_op jit(solution)/shard_map/psum | solution.py:73
  142.2 1.4 copy.120
  145.2 4.0 collective-permute-start.7
  150.0 1.8 collective-permute-start.11
  153.9 3.4 collective-permute-start.8
  157.4 3.0 collective-permute-start.9
  162.3 5.0 %add_bitcast_fusion.3 = (f32[1,6,128,128]{3,2,1,0:T(8,128)S(1)}, f32[6,128,128]{2,1,0:T(8,128)S(1)}, f32[6,128,128]{2,1,0:T(8,128)S(1)}, f32[6,128,128]{2,1,0:T(...) fusion(f32[2,6,128,128]{3,2,1,0:T(8,128)S(1)} %multiply_add_fusion.2, ...), kind=kLoop, calls=%fused_computation.263 | loop fusion | flops 19169280 | bytes 11534336 | tf_op jit(solution)/shard_map/stack | solution.py:63
  167.4 4.8 %add_bitcast_fusion.2 = f32[1,6,128,128]{3,2,1,0:T(8,128)S(1)} fusion(f32[6,128,128]{2,1,0:T(8,128)S(1)} %get-tuple-element.21, f32[6,128,128]{2,1,0:T(8,128)S(1)} %get-tuple-element.20, f32[6,128,128]{2,1,0:T(8,128)S(1)} %get-tuple-element.19, f32[6,128,128]{2,1,0:T(8,128)S(1)} %get-tuple-element.18, f32[2,6,129,130]{3,2,1,0:T(8,128)S(1)} %get-tuple-element.34, ...), kind=kLoop, calls=%fused_computation.262 | loop fusion | flops 17793024 | bytes 9961472 | tf_op jit(solution)/shard_map/stack | solution.py:63
  173.7 97.1 %psum.22 = f32[]{:T(128)} all-reduce(f32[]{:T(128)S(6)} %mul.751), channel_id=1, replica_groups=mesh['gx'=8,'gy'=8,'gz'=8] {'gx','gy','gz'}, use_global_device_ids=true, to_apply=%region_3.4 | all-reduce | flops 1 | bytes 8 | tf_op jit(solution)/shard_map/psum | solution.py:73
  273.8 4.0 collective-permute-start.13
  278.6 3.5 collective-permute-start.17
  284.1 3.4 collective-permute-start.14
  287.6 4.2 %collective-permute-start.15 = (f32[2,6,1,130]{3,0,2,1:T(2,128)S(1)}, f32[2,6,1,130]{3,0,2,1:T(2,128)S(1)}, u32[]{:S(2)}, u32[]{:S(2)}) collective-permute-start(f32[2,6,1,130]{3,0,2,1:T(2,128)S(1)} %copy.136), channel_id=1, source_target_pairs={{0,8},{8,16},{16,24},{24,32},{32,40},{40,48},{48,56},{1,9},{9,17},... | collective-permute-start | bytes 18728 | tf_op jit(solution)/shard_map/ppermute | solution.py:27
  293.7 5.1 %add_bitcast_fusion.1 = (f32[1,6,128,128]{3,2,1,0:T(8,128)S(1)}, f32[6,128,128]{2,1,0:T(8,128)S(1)}, f32[6,128,128]{2,1,0:T(8,128)S(1)}, f32[6,128,128]{2,1,0:T(...) fusion(f32[2,6,128,128]{3,2,1,0:T(8,128)S(1)} %multiply_add_fusion.1, ...), kind=kLoop, calls=%fused_computation.249 | loop fusion | flops 19169280 | bytes 11534336 | tf_op jit(solution)/shard_map/stack | solution.py:63
  298.9 4.9 %add_bitcast_fusion = f32[1,6,128,128]{3,2,1,0:T(8,128)S(1)} fusion(f32[6,128,128]{2,1,0:T(8,128)S(1)} %get-tuple-element.12, f32[6,128,128]{2,1,0:T(8,128)S(1)} %get-tuple-element.11, f32[6,128,128]{2,1,0:T(8,128)S(1)} %get-tuple-element.10, f32[6,128,128]{2,1,0:T(8,128)S(1)} %get-tuple-element.9, f32[2,6,129,130]{3,2,1,0:T(8,128)S(1)} %get-tuple-element.30, ...), kind=kLoop, calls=%fused_computation.248 | loop fusion | flops 17793024 | bytes 9961472 | tf_op jit(solution)/shard_map/stack | solution.py:63
  305.3 97.3 %psum.23 = f32[]{:T(128)} all-reduce(f32[]{:T(128)S(6)} %mul.815), channel_id=1, replica_groups=mesh['gx'=8,'gy'=8,'gz'=8] {'gx','gy','gz'}, use_global_device_ids=true, to_apply=%region_5.6 | all-reduce | flops 1 | bytes 8 | tf_op jit(solution)/shard_map/psum | solution.py:73
  403.3 2.4 multiply_add_fusion
  (85 shorter events, 25.5 us)
Async XLA Ops:
  0.6 8.4 %copy-start = (f32[2,6,128,128]{3,2,1,0:T(8,128)S(1)}, f32[2,6,128,128]{3,2,1,0:T(8,128)}, u32[]{:S(2)}) copy-start(f32[2,6,128,128]{3,2,1,0:T(8,128)} %param.4) | copy-start | bytes 2359300
  2.8 13.5 %collective-permute-start = (f32[2,6,128,1]{2,0,3,1:T(2,128)S(1)}, f32[2,6,128,1]{2,0,3,1:T(2,128)S(1)}, u32[]{:S(2)}, u32[]{:S(2)}) collective-permute-start(f32[2,6,128,1]{2,0,3,1:T(2,128)S(1)} %copy.138), channel_id=1, source_target_pairs={{64,0},{128,64},{192,128},{256,192},{320,256},{384,320},{448,384},... | collective-permute-start | bytes 18440 | tf_op jit(solution)/shard_map/ppermute | solution.py:30
  4.3 11.6 %collective-permute-start.1 = (f32[2,6,128,1]{2,0,3,1:T(2,128)S(1)}, f32[2,6,128,1]{2,0,3,1:T(2,128)S(1)}, u32[]{:S(2)}, u32[]{:S(2)}) collective-permute-start(f32[2,6,128,1]{2,0,3,1:T(2,128)S(1)} %copy.139), channel_id=1, source_target_pairs={{0,64},{64,128},{128,192},{192,256},{256,320},{320,384},{384,448},... | collective-permute-start | bytes 18440 | tf_op jit(solution)/shard_map/ppermute | solution.py:27
  9.8 17.2 %collective-permute-start.5 = (f32[2,2,128,128]{3,2,1,0:T(8,128)}, f32[2,2,128,128]{3,2,1,0:T(8,128)}, u32[]{:S(2)}, u32[]{:S(2)}) collective-permute-start(f32[2,2,128,128]{3,2,1,0:T(8,128)} %get-tuple-element.53), channel_id=1, source_target_pairs={{0,1},{1,2},{2,3},{3,4},{4,5},{5,6},{6,7},{8,9},{9,10},{10,11},{11... | collective-permute-start | bytes 786440 | tf_op jit(solution)/shard_map/ppermute | solution.py:27
  14.7 13.6 %collective-permute-start.4 = (f32[2,2,128,128]{3,2,1,0:T(8,128)}, f32[2,2,128,128]{3,2,1,0:T(8,128)S(1)}, u32[]{:S(2)}, u32[]{:S(2)}) collective-permute-start(f32[2,2,128,128]{3,2,1,0:T(8,128)} %get-tuple-element.54), channel_id=1, source_target_pairs={{1,0},{2,1},{3,2},{4,3},{5,4},{6,5},{7,6},{9,8},{10,9},{11,10},{12... | collective-permute-start | bytes 786440 | tf_op jit(solution)/shard_map/ppermute | solution.py:30
  16.3 8.3 %copy-start.8 = (s32[6,128,128]{2,1,0:T(8,128)S(1)}, s32[6,128,128]{2,1,0:T(8,128)}, u32[]{:S(2)}) copy-start(s32[6,128,128]{2,1,0:T(8,128)} %param.7) | copy-start | bytes 1179652
  16.8 7.8 %collective-permute-start.2 = (f32[2,6,1,130]{3,0,2,1:T(2,128)S(1)}, f32[2,6,1,130]{3,0,2,1:T(2,128)S(1)}, u32[]{:S(2)}, u32[]{:S(2)}) collective-permute-start(f32[2,6,1,130]{3,0,2,1:T(2,128)S(1)} %copy.114), channel_id=1, source_target_pairs={{8,0},{16,8},{24,16},{32,24},{40,32},{48,40},{56,48},{9,1},{17,9},... | collective-permute-start | bytes 18728 | tf_op jit(solution)/shard_map/ppermute | solution.py:30
  22.6 3.1 collective-permute-start.3
  24.6 147.6 %copy-start.2 = (f32[6,128,128]{2,1,0:T(8,128)}, f32[6,128,128]{2,1,0:T(8,128)S(1)}, u32[]{:S(2)}) copy-start(f32[6,128,128]{2,1,0:T(8,128)S(1)} %subtract_convert_fusion) | copy-start | bytes 1179652
  37.1 105.1 %copy-start.4 = (f32[2,6,128,128]{3,2,1,0:T(8,128)}, f32[2,6,128,128]{3,2,1,0:T(8,128)S(1)}, u32[]{:S(2)}) copy-start(f32[2,6,128,128]{3,2,1,0:T(8,128)S(1)} %get-tuple-element.23) | copy-start | bytes 2359300
  143.9 9.6 %collective-permute-start.6 = (f32[2,6,128,1]{2,0,3,1:T(2,128)S(1)}, f32[2,6,128,1]{2,0,3,1:T(2,128)S(1)}, u32[]{:S(2)}, u32[]{:S(2)}) collective-permute-start(f32[2,6,128,1]{2,0,3,1:T(2,128)S(1)} %copy.118), channel_id=1, source_target_pairs={{64,0},{128,64},{192,128},{256,192},{320,256},{384,320},{448,384},... | collective-permute-start | bytes 18440 | tf_op jit(solution)/shard_map/ppermute | solution.py:30
  145.2 8.0 %collective-permute-start.7 = (f32[2,6,128,1]{2,0,3,1:T(2,128)S(1)}, f32[2,6,128,1]{2,0,3,1:T(2,128)S(1)}, u32[]{:S(2)}, u32[]{:S(2)}) collective-permute-start(f32[2,6,128,1]{2,0,3,1:T(2,128)S(1)} %copy.120), channel_id=1, source_target_pairs={{0,64},{64,128},{128,192},{192,256},{256,320},{320,384},{384,448},... | collective-permute-start | bytes 18440 | tf_op jit(solution)/shard_map/ppermute | solution.py:27
  150.0 12.3 %collective-permute-start.11 = (f32[2,2,128,128]{3,2,1,0:T(8,128)}, f32[2,2,128,128]{3,2,1,0:T(8,128)S(1)}, u32[]{:S(2)}, u32[]{:S(2)}) collective-permute-start(f32[2,2,128,128]{3,2,1,0:T(8,128)} %get-tuple-element.45), channel_id=1, source_target_pairs={{0,1},{1,2},{2,3},{3,4},{4,5},{5,6},{6,7},{8,9},{9,10},{10,11},{11... | collective-permute-start | bytes 786440 | tf_op jit(solution)/shard_map/ppermute | solution.py:27
  151.8 10.5 %collective-permute-start.10 = (f32[2,2,128,128]{3,2,1,0:T(8,128)}, f32[2,2,128,128]{3,2,1,0:T(8,128)}, u32[]{:S(2)}, u32[]{:S(2)}) collective-permute-start(f32[2,2,128,128]{3,2,1,0:T(8,128)} %get-tuple-element.46), channel_id=1, source_target_pairs={{1,0},{2,1},{3,2},{4,3},{5,4},{6,5},{7,6},{9,8},{10,9},{11,10},{12... | collective-permute-start | bytes 786440 | tf_op jit(solution)/shard_map/ppermute | solution.py:30
  153.9 6.4 %collective-permute-start.8 = (f32[2,6,1,130]{3,0,2,1:T(2,128)S(1)}, f32[2,6,1,130]{3,0,2,1:T(2,128)S(1)}, u32[]{:S(2)}, u32[]{:S(2)}) collective-permute-start(f32[2,6,1,130]{3,0,2,1:T(2,128)S(1)} %copy.124), channel_id=1, source_target_pairs={{8,0},{16,8},{24,16},{32,24},{40,32},{48,40},{56,48},{9,1},{17,9},... | collective-permute-start | bytes 18728 | tf_op jit(solution)/shard_map/ppermute | solution.py:30
  157.4 3.6 collective-permute-start.9
  272.5 11.2 %collective-permute-start.12 = (f32[2,6,128,1]{2,0,3,1:T(2,128)S(1)}, f32[2,6,128,1]{2,0,3,1:T(2,128)S(1)}, u32[]{:S(2)}, u32[]{:S(2)}) collective-permute-start(f32[2,6,128,1]{2,0,3,1:T(2,128)S(1)} %copy.128), channel_id=1, source_target_pairs={{64,0},{128,64},{192,128},{256,192},{320,256},{384,320},{448,384},... | collective-permute-start | bytes 18440 | tf_op jit(solution)/shard_map/ppermute | solution.py:30
  273.8 9.6 %collective-permute-start.13 = (f32[2,6,128,1]{2,0,3,1:T(2,128)S(1)}, f32[2,6,128,1]{2,0,3,1:T(2,128)S(1)}, u32[]{:S(2)}, u32[]{:S(2)}) collective-permute-start(f32[2,6,128,1]{2,0,3,1:T(2,128)S(1)} %copy.130), channel_id=1, source_target_pairs={{0,64},{64,128},{128,192},{192,256},{256,320},{320,384},{384,448},... | collective-permute-start | bytes 18440 | tf_op jit(solution)/shard_map/ppermute | solution.py:27
  278.6 15.1 %collective-permute-start.17 = (f32[2,2,128,128]{3,2,1,0:T(8,128)}, f32[2,2,128,128]{3,2,1,0:T(8,128)}, u32[]{:S(2)}, u32[]{:S(2)}) collective-permute-start(f32[2,2,128,128]{3,2,1,0:T(8,128)} %get-tuple-element.41), channel_id=1, source_target_pairs={{0,1},{1,2},{2,3},{3,4},{4,5},{5,6},{6,7},{8,9},{9,10},{10,11},{11... | collective-permute-start | bytes 786440 | tf_op jit(solution)/shard_map/ppermute | solution.py:27
  282.1 11.7 %collective-permute-start.16 = (f32[2,2,128,128]{3,2,1,0:T(8,128)}, f32[2,2,128,128]{3,2,1,0:T(8,128)}, u32[]{:S(2)}, u32[]{:S(2)}) collective-permute-start(f32[2,2,128,128]{3,2,1,0:T(8,128)} %get-tuple-element.42), channel_id=1, source_target_pairs={{1,0},{2,1},{3,2},{4,3},{5,4},{6,5},{7,6},{9,8},{10,9},{11,10},{12... | collective-permute-start | bytes 786440 | tf_op jit(solution)/shard_map/ppermute | solution.py:30
  284.1 7.6 %collective-permute-start.14 = (f32[2,6,1,130]{3,0,2,1:T(2,128)S(1)}, f32[2,6,1,130]{3,0,2,1:T(2,128)S(1)}, u32[]{:S(2)}, u32[]{:S(2)}) collective-permute-start(f32[2,6,1,130]{3,0,2,1:T(2,128)S(1)} %copy.134), channel_id=1, source_target_pairs={{8,0},{16,8},{24,16},{32,24},{40,32},{48,40},{56,48},{9,1},{17,9},... | collective-permute-start | bytes 18728 | tf_op jit(solution)/shard_map/ppermute | solution.py:30
  287.6 4.8 %collective-permute-start.15 = (f32[2,6,1,130]{3,0,2,1:T(2,128)S(1)}, f32[2,6,1,130]{3,0,2,1:T(2,128)S(1)}, u32[]{:S(2)}, u32[]{:S(2)}) collective-permute-start(f32[2,6,1,130]{3,0,2,1:T(2,128)S(1)} %copy.136), channel_id=1, source_target_pairs={{0,8},{8,16},{16,24},{24,32},{32,40},{40,48},{48,56},{1,9},{9,17},... | collective-permute-start | bytes 18728 | tf_op jit(solution)/shard_map/ppermute | solution.py:27
  298.8 5.0 %copy-start.6 = (f32[1,6,128,128]{3,2,1,0:T(8,128)}, f32[1,6,128,128]{3,2,1,0:T(8,128)S(1)}, u32[]{:S(2)}) copy-start(f32[1,6,128,128]{3,2,1,0:T(8,128)S(1)} %get-tuple-element.6) | copy-start | bytes 1179652
  298.8 5.0 %copy-start.3 = (f32[6,128,128]{2,1,0:T(8,128)S(1)}, f32[6,128,128]{2,1,0:T(8,128)}, u32[]{:S(2)}) copy-start(f32[6,128,128]{2,1,0:T(8,128)} %copy-done.2) | copy-start | bytes 1179652
  (3 other events, 9.9 us)
where the time goes:
time: 407 us; the launch traced here: 406 us
  blocking collectives  297 us (73%)
  starting transfers between devices  52.2 us (13%)
  other arithmetic  37.3 us (9%)
  local copies, waits for them, and re-layouts  11.7 us (3%)
  between operations  5.42 us (1%)
    psum x3, blocking collectives, total_energy(): return lax.psum(0.5 * jnp.sum(kicked * kicked), ('gx', 'gy', 'gz'))  297 us
    ppermute x9, starting transfers between devices, extended(): lax.ppermute(lax.slice_in_dim(block, block.shape[dim] - width, None, axis...  31.9 us
    another operation x6, other arithmetic, spring_force(): return jnp.stack([force_y, force_x])  27.8 us
    ppermute x9, starting transfers between devices, extended(): lax.ppermute(lax.slice_in_dim(block, 0, width, axis=dim), axis, backward)  20.4 us
  transfers between devices with their start and end apart: 18, of which 3 were waited for; matrix products, arithmetic and copies ran while one was open for 3% of the time, Pallas kernels for 0%

commit v1 on v0

v1 whole, which is shorter than its diff:
```python
import functools
import itertools
import math

import jax
import jax.numpy as jnp
from jax import lax
from jax.experimental import pallas as pl
from jax.experimental.pallas import tpu as pltpu
from jax.sharding import PartitionSpec as P

MESH = pl.DeviceIdType.MESH
ITERS = 3
TIME_STEP = 0.3
DAMPING = 0.9
STIFF_PLANE = 1.0
HUBER_DELTA = 0.5
LENGTH_FLOOR = 0.25
ENERGY_CAP = 0.04
EPSILON = 1e-06
DIAG = math.sqrt(2.0)
AXES = ("gx", "gy", "gz")
F32 = jnp.float32

COLUMN_PEERS = ((1, 0), (-1, 0), (1, 1), (-1, 1), (1, -1), (-1, -1))
FROM_LEFT, FROM_RIGHT, FROM_UP_LEFT, FROM_UP_RIGHT, FROM_DOWN_LEFT, FROM_DOWN_RIGHT = range(6)


def lanes_left(a):
    return pltpu.roll(a, 127, 1)


def lanes_right(a):
    return pltpu.roll(a, 1, 1)


def plane_weight(dy, dx, rest, mask):
    square = dy * dy + dx * dx
    u = jnp.minimum(lax.rsqrt(square), 1.0 / LENGTH_FLOOR)
    stretch = jnp.clip(square * u - rest, -HUBER_DELTA, HUBER_DELTA)
    return stretch * u * mask


def depth_weight(dy, dx, mask):
    square = dy * dy + dx * dx
    return jnp.minimum(lax.rsqrt(square), 1.0 / HUBER_DELTA) * mask


def bit(codes, index, scale):
    return jnp.where((codes & (1 << index)) != 0, F32(scale), F32(0.0))


def kernel(sizes, comm, *refs):
    (pos_in, vel_in, code_in, fix_in, pos_out, kick_out, fac_out,
     pos, rolled, kick, force, below, below_right, codes, fixed, m_plane, m_one, m_two, mov,
     z_in, edge_own, edge_in, row_own, row_in, edge_pos, edge_halo, row_pos, up_pos, down_pos,
     m_edge, m_top, edge_force, sum_src, sum_a, sum_b,
     load_sem, out_sem, halo_send, halo_recv, sum_send, sum_recv) = refs
    nx, ny, nz, nodes_all = sizes
    chips = ny // 2
    me = {a: lax.axis_index(a) for a in AXES}

    def shifted(ox, oy, oz):
        return (lax.rem(me["gx"] + ox + nx, nx), lax.rem(me["gy"] + oy + ny, ny), lax.rem(me["gz"] + oz + nz, nz))

    def by_chip(ox, chip, core, oz):
        gy = me["gy"]
        where = lax.rem(lax.div(gy, 2) + chip, chips) * 2 + lax.rem(lax.rem(gy, 2) + core, 2)
        return (lax.rem(me["gx"] + ox, nx), where, lax.rem(me["gz"] + oz, nz))

    def far(o):
        ox, chip, core, oz = o
        return -(min(ox, nx - ox) + min(chip, chips - chip) + min(oz, nz - oz)) - 0.1 * core

    group_a = sorted([(i, 0, c, 0) for i in range(nx) for c in range(2) if i or c], key=far)
    group_b = sorted([(0, c, 0, k) for c in range(chips) for k in range(nz) if c or k], key=far)

    loads = [
        pltpu.make_async_copy(pos_in, pos.at[:, :, pl.ds(0, 128), :], load_sem.at[0]),
        pltpu.make_async_copy(code_in, codes, load_sem.at[1]),
        pltpu.make_async_copy(vel_in, kick, load_sem.at[2]),
        pltpu.make_async_copy(fix_in, fixed, load_sem.at[3]),
    ]
    for c in loads:
        c.start()

    if comm:
        barrier = pltpu.get_barrier_semaphore()
        near = [shifted(0, 1, 0), shifted(0, -1, 0)] + [shifted(i, j, 0) for i in (1, -1) for j in (1, -1)]
        peers = near + [by_chip(*o) for o in group_a + group_b]
        for peer in peers:
            pl.semaphore_signal(barrier, inc=1, device_id=peer, device_id_type=MESH)

    lane = lax.broadcasted_iota(jnp.int32, (8, 128), 1)
    is_last = lane == 127
    is_first = lane == 0
    is_edge = is_last | is_first
    pair = [(lane >> 1) == z for z in range(6)]
    odd16 = (lax.broadcasted_iota(jnp.int32, (16, 128), 1) & 1) == 1
    odd8 = (lane & 1) == 1
    group_of = lane >> 4
    zero = jnp.zeros((8, 128), F32)

    def gather_edges(values, g):
        packed = jnp.zeros_like(values[0])
        for z in range(6):
            packed = jnp.where(pair[z], pltpu.roll(values[z], 2 * z + 1, 1), packed)
        return pltpu.roll(packed, 16 * g, 1)

    def pack_rows(it, source):
        for c in range(2):
            for z in range(6):
                row_own[it, 0, c, z:z + 1, :] = source[c, z, 0:1, :]
                row_own[it, 1, c, z:z + 1, :] = source[c, z, 127:128, :]

    def halo_copies(it, source):
        out = []
        for side, (oz, first) in enumerate(((1, 4), (-1, 0))):
            out.append((source.at[:, pl.ds(first, 2), pl.ds(0, 128), :], z_in.at[it, side], shifted(0, 0, oz)))
        for side, (oy, which) in enumerate(((1, 1), (-1, 0))):
            out.append((row_own.at[it, which], row_in.at[it, side], shifted(0, oy, 0)))
        for slot, (ox, oy) in enumerate(COLUMN_PEERS):
            out.append((edge_own.at[it], edge_in.at[it, slot], shifted(ox, oy, 0)))
        return [
            pltpu.make_async_remote_copy(
                src_ref=s, dst_ref=d, send_sem=halo_send.at[it, n], recv_sem=halo_recv.at[it, n],
                device_id=peer, device_id_type=MESH)
            for n, (s, d, peer) in enumerate(out)
        ]

    def send_sum(it, phase, group, buffer, value):
        if not comm:
            return
        sum_src[it, phase] = value
        for k, o in enumerate(group, 1):
            pltpu.make_async_remote_copy(
                src_ref=sum_src.at[it, phase], dst_ref=buffer.at[it, k],
                send_sem=sum_send.at[it, phase], recv_sem=sum_recv.at[it, phase],
                device_id=by_chip(*o), device_id_type=MESH).start()

    def take_sum(it, phase, group, buffer, value):
        if not comm:
            return value
        got = buffer.at[it, pl.ds(1, len(group))]
        pltpu.make_async_remote_copy(
            src_ref=got, dst_ref=got, send_sem=sum_send.at[it, phase], recv_sem=sum_recv.at[it, phase],
            device_id=by_chip(*group[0]), device_id_type=MESH).wait_recv()
        for k in range(1, len(group) + 1):
            value = value + buffer[it, k]
        return value

    def wait_sums_sent(it):
        for phase, (group, buffer) in enumerate(((group_a, sum_a), (group_b, sum_b))):
            got = buffer.at[it, pl.ds(1, len(group))]
            pltpu.make_async_remote_copy(
                src_ref=got, dst_ref=got, send_sem=sum_send.at[it, phase], recv_sem=sum_recv.at[it, phase],
                device_id=by_chip(*group[0]), device_id_type=MESH).wait_send()

    row_own[...] = jnp.zeros_like(row_own)
    loads[0].wait()
    pack_rows(0, pos)

    def pack_positions(g, packed):
        out = list(packed)
        for j in range(2):
            r = pl.multiple_of(16 * g + 8 * j, 8)
            for c in range(2):
                values = [pos[c, z, pl.ds(r, 8), :] for z in range(6)]
                out[2 * c + j] = out[2 * c + j] + gather_edges(values, g)
        return tuple(out)

    packed = lax.fori_loop(0, 8, pack_positions, (zero,) * 4, unroll=4)
    for c in range(2):
        for j in range(2):
            edge_own[0, c, 8 * j:8 * j + 8, :] = packed[2 * c + j]

    if comm:
        pl.semaphore_wait(barrier, len(peers))
        copies = [halo_copies(0, pos)]
        for c in copies[0]:
            c.start()

    loads[1].wait()
    loads[3].wait()
    plane = TIME_STEP * STIFF_PLANE
    one = TIME_STEP * HUBER_DELTA * 0.5
    two = TIME_STEP * HUBER_DELTA * 0.25

    def masks(g, packed):
        out = list(packed)
        for j in range(2):
            r = pl.multiple_of(16 * g + 8 * j, 8)
            rows = pl.ds(r, 8)
            kept = []
            for z in range(6):
                code = codes[z, rows, :]
                kept.append(code)
                m_plane[0, z, rows, :] = jnp.where(is_last, 0.0, bit(code, 0, plane))
                m_plane[1, z, rows, :] = bit(code, 2, plane)
                m_plane[2, z, rows, :] = jnp.where(is_last, 0.0, bit(code, 4, plane))
                m_plane[3, z, rows, :] = jnp.where(is_last, 0.0, lanes_left(bit(code, 6, plane)))
                m_one[z + 1, rows, :] = bit(code, 8, one)
                m_two[z + 2, rows, :] = bit(code, 10, two)
                if z == 0:
                    m_one[0, rows, :] = bit(code, 9, one)
                if z < 2:
                    m_two[z, rows, :] = bit(code, 11, two)
                mov[z, rows, :] = (1 - fixed[z, rows, :]).astype(F32)
            out[j] = out[j] + gather_edges(kept, g)
        return tuple(out)

    edge_codes = lax.fori_loop(0, 8, masks, (jnp.zeros((8, 128), jnp.int32),) * 2, unroll=2)
    for j in range(2):
        for n, (first, last) in enumerate(((5, 7), (1, 0), (6, 4))):
            m_edge[n, 8 * j:8 * j + 8, :] = jnp.where(odd8, bit(edge_codes[j], first, plane), bit(edge_codes[j], last, plane))
    for z in range(6):
        code = codes[z, 0:1, :]
        line = lax.broadcasted_iota(jnp.int32, (1, 128), 1)
        m_top[0, z:z + 1, :] = bit(code, 3, plane)
        m_top[1, z:z + 1, :] = jnp.where(line == 127, 0.0, bit(code, 7, plane))
        m_top[2, z:z + 1, :] = jnp.where(line == 0, 0.0, bit(code, 5, plane))

    def build_halo(it, c):
        def got(slot, j):
            return edge_in[it, slot, c, 8 * j:8 * j + 8, :]

        near_rows = [jnp.where(odd8, lanes_right(got(FROM_LEFT, j)), lanes_left(got(FROM_RIGHT, j))) for j in range(2)]
        up = jnp.where(odd8, pltpu.roll(got(FROM_UP_LEFT, 1), 17, 1), pltpu.roll(got(FROM_UP_RIGHT, 1), 15, 1))
        down = jnp.where(odd8, pltpu.roll(got(FROM_DOWN_LEFT, 0), 113, 1), pltpu.roll(got(FROM_DOWN_RIGHT, 0), 111, 1))
        above = jnp.where(group_of == 0, up, pltpu.roll(near_rows[1], 16, 1))
        under = jnp.where(group_of == 7, down, pltpu.roll(near_rows[0], 112, 1))
        return [above, near_rows[0], near_rows[1], under]

    loads[2].wait()
    scale = None
    damp = F32(DAMPING)
    for it in range(ITERS):
        first = it == 0

        def advance(z, carry):
            for i in range(16):
                rows = slice(8 * i, 8 * i + 8)
                for c in range(2):
                    p = pos[c, z, rows, :]
                    if not first:
                        p = p + scale * kick[c, z, rows, :]
                        pos[c, z, rows, :] = p
                    p = lanes_left(p)
                    rolled[c, z, rows, :] = p + 1.0 if c else p
            return carry

        lax.fori_loop(0, 6, advance, 0, unroll=6)

        if comm:
            for n in range(2, 10):
                copies[it][n].wait_recv()

        for c in range(2):
            own, up, down = row_own[it, 0, c], row_in[it, 0, c], row_in[it, 1, c]
            edges = edge_own[it, c]
            halo = build_halo(it, c)
            if not first:
                own = row_pos[c] + scale * own
                up = up_pos[c] + scale * up
                down = down_pos[c] + scale * down
                edges = edge_pos[c] + jnp.concatenate([scale, scale], 0) * edges
                halo = [edge_halo[c, 8 * n:8 * n + 8, :] + scale * h for n, h in enumerate(halo)]
            row_pos[c], up_pos[c], down_pos[c], edge_pos[c] = own, up, down, edges
            for n, h in enumerate(halo):
                edge_halo[c, 8 * n:8 * n + 8, :] = h
            right = lanes_left(down)
            right = right + 1.0 if c else right
            for z in range(6):
                pos[c, z, 128:129, :] = down[z:z + 1, :]
                rolled[c, z, 128:129, :] = right[z:z + 1, :]

        top = [zero, zero]
        own_y, own_x, up_y, up_x = row_pos[0], row_pos[1], up_pos[0], up_pos[1]
        for n, (step, turn) in enumerate(((0, 0), (1, 127), (-1, 1))):
            ny_, nx_ = (pltpu.roll(up_y, turn, 1), pltpu.roll(up_x, turn, 1)) if turn else (up_y, up_x)
            dy, dx = ny_ - own_y - 1.0, nx_ - own_x + float(step)
            w = plane_weight(dy, dx, DIAG if step else 1.0, m_top[n])
            top = [top[0] + w * dy, top[1] + w * dx]
        for c in range(2):
            for z in range(6):
                below[c, z, 7:8, :] = -top[c][z:z + 1, :]
                below_right[c, z, 7:8, :] = jnp.zeros((1, 128), F32)

        side = [jnp.zeros((16, 128), F32)] * 2
        way = jnp.where(odd16, F32(-1.0), F32(1.0))
        own_y, own_x = edge_pos[0], edge_pos[1]
        for n, step in enumerate((-1, 0, 1)):
            dy = edge_halo[0, 8 + step:24 + step, :] - own_y + float(step)
            dx = edge_halo[1, 8 + step:24 + step, :] - own_x + way
            w = plane_weight(dy, dx, DIAG if step else 1.0, m_edge[n])
            side = [side[0] + w * dy, side[1] + w * dx]
        for c in range(2):
            edge_force[c] = side[c]

        def in_plane(z, carry):
            for i in range(16):
                r = 8 * i
                rows, next_rows = slice(r, r + 8), slice(r + 1, r + 9)
                y, x = pos[0, z, rows, :], pos[1, z, rows, :]
                y_d, x_d = pos[0, z, next_rows, :], pos[1, z, next_rows, :]
                y_r, x_r = rolled[0, z, rows, :], rolled[1, z, rows, :]
                y_dr, x_dr = rolled[0, z, next_rows, :], rolled[1, z, next_rows, :]
                y_less, y_r_less = y - 1.0, y_r - 1.0

                def link(dy, dx, rest, n):
                    w = plane_weight(dy, dx, rest, m_plane[n, z, rows, :])
                    return w * dy, w * dx

                across = link(y_r - y, x_r - x, 1.0, 0)
                down = link(y_d - y_less, x_d - x, 1.0, 1)
                diag = link(y_dr - y_less, x_dr - x, DIAG, 2)
                anti = link(y_d - y_r_less, x_d - x_r, DIAG, 3)
                for c in range(2):
                    below[c, z, r + 8:r + 16, :] = down[c] + anti[c]
                    below_right[c, z, r + 8:r + 16, :] = diag[c]
                    here = across[c] + down[c] + diag[c] - below[c, z, r + 7:r + 15, :]
                    right = anti[c] - across[c] - below_right[c, z, r + 7:r + 15, :]
                    force[c, z, rows, :] = here + lanes_right(right)
            return carry

        lax.fori_loop(0, 6, in_plane, 0)

        if comm:
            for n in range(2):
                copies[it][n].wait()

        def depth(g, carry):
            energy, packed = carry[0], list(carry[1:])
            for j in range(2):
                r = pl.multiple_of(16 * g + 8 * j, 8)
                rows = pl.ds(r, 8)
                at, got = {}, {}
                for z in range(6):
                    at[z] = [pos[c, z, rows, :] for c in range(2)]
                    got[z] = [force[c, z, rows, :] for c in range(2)]
                for s in range(2):
                    for n in range(2):
                        vals = []
                        for c in range(2):
                            v = z_in[0, s, c, n, rows, :]
                            if not first:
                                v = v + scale * z_in[it, s, c, n, rows, :]
                                if it < ITERS - 1:
                                    z_in[0, s, c, n, rows, :] = v
                            vals.append(v)
                        at[n - 2 if s == 0 else n + 6] = vals
                for reach, mask in ((1, m_one), (2, m_two)):
                    for z in range(-reach, 6):
                        a, b = at[z], at[z + reach]
                        dy, dx = b[0] - a[0], b[1] - a[1]
                        w = depth_weight(dy, dx, mask[z + reach, rows, :])
                        for c, d in enumerate((w * dy, w * dx)):
                            if z >= 0:
                                got[z][c] = got[z][c] + d
                            if z + reach < 6:
                                got[z + reach][c] = got[z + reach][c] - d
                kicked = [[], []]
                for c in range(2):
                    edge = pltpu.roll(edge_force[c, 8 * j:8 * j + 8, :], lax.rem(128 - 16 * g, 128), 1)
                    for z in range(6):
                        f = got[z][c] + jnp.where(is_edge, pltpu.roll(edge, 127 - 2 * z, 1), 0.0)
                        k = (damp * kick[c, z, rows, :] + f) * mov[z, rows, :]
                        kick[c, z, rows, :] = k
                        energy = energy + k * k
                        kicked[c].append(k)
                    if it < ITERS - 1:
                        packed[2 * c + j] = packed[2 * c + j] + gather_edges(kicked[c], g)
            return (energy, *packed)

        energy, *packed = lax.fori_loop(0, 8, depth, (zero,) * 5, unroll=4)

        if it < ITERS - 1:
            pack_rows(it + 1, kick)
            for c in range(2):
                for j in range(2):
                    edge_own[it + 1, c, 8 * j:8 * j + 8, :] = packed[2 * c + j]

        total = jnp.sum(energy, axis=0, keepdims=True)
        send_sum(it, 0, group_a, sum_a, total)
        if comm and it < ITERS - 1:
            copies.append(halo_copies(it + 1, kick))
            for c in copies[it + 1]:
                c.start()
        if it == ITERS - 1:
            outs = [
                pltpu.make_async_copy(pos.at[:, :, pl.ds(0, 128), :], pos_out, out_sem.at[0]),
                pltpu.make_async_copy(kick, kick_out, out_sem.at[1]),
            ]
            for c in outs:
                c.start()
        total = take_sum(it, 0, group_a, sum_a, total)
        send_sum(it, 1, group_b, sum_b, total)
        total = take_sum(it, 1, group_b, sum_b, total)
        kinetic = 0.5 * jnp.sum(total, axis=1, keepdims=True)
        factor = jnp.minimum(1.0, jnp.sqrt(ENERGY_CAP * nodes_all / (kinetic + EPSILON)))
        factor = jnp.broadcast_to(factor, (8, 128))
        scale = TIME_STEP * factor
        damp = DAMPING * factor

    fac_out[...] = factor
    for c in outs:
        c.wait()
    if comm:
        for it in range(ITERS):
            for c in copies[it][2:]:
                c.wait_send()
            wait_sums_sent(it)


def local(sizes, comm, positions, velocities, link_codes, fixed_nodes):
    nx, ny, nz = sizes
    _, deep, rows, cols = positions.shape
    assert (deep, rows, cols) == (6, 128, 128)
    nodes_all = deep * rows * cols * nx * ny * nz
    vmem = pltpu.VMEM
    block = (2, 6, 128, 128)
    scratch = [
        vmem((2, 6, 136, 128), F32),
        vmem((2, 6, 136, 128), F32),
        vmem(block, F32),
        vmem(block, F32),
        vmem((2, 6, 136, 128), F32),
        vmem((2, 6, 136, 128), F32),
        vmem((6, 128, 128), jnp.int32),
        vmem((6, 128, 128), jnp.int32),
        vmem((4, 6, 128, 128), F32),
        vmem((7, 128, 128), F32),
        vmem((8, 128, 128), F32),
        vmem((6, 128, 128), F32),
        vmem((ITERS, 2, 2, 2, 128, 128), F32),
        vmem((ITERS, 2, 16, 128), F32),
        vmem((ITERS, 6, 2, 16, 128), F32),
        vmem((ITERS, 2, 2, 8, 128), F32),
        vmem((ITERS, 2, 2, 8, 128), F32),
        vmem((2, 16, 128), F32),
        vmem((2, 32, 128), F32),
        vmem((2, 8, 128), F32),
        vmem((2, 8, 128), F32),
        vmem((2, 8, 128), F32),
        vmem((3, 16, 128), F32),
        vmem((3, 8, 128), F32),
        vmem((2, 16, 128), F32),
        vmem((ITERS, 2, 1, 128), F32),
        vmem((ITERS, 2 * nx, 1, 128), F32),
        vmem((ITERS, ny // 2 * nz, 1, 128), F32),
        pltpu.SemaphoreType.DMA((4,)),
        pltpu.SemaphoreType.DMA((2,)),
        pltpu.SemaphoreType.DMA((ITERS, 10)),
        pltpu.SemaphoreType.DMA((ITERS, 10)),
        pltpu.SemaphoreType.DMA((ITERS, 2)),
        pltpu.SemaphoreType.DMA((ITERS, 2)),
    ]
    anywhere = pl.BlockSpec(memory_space=pltpu.MemorySpace.HBM)
    position, kicked, factor = pl.pallas_call(
        functools.partial(kernel, (nx, ny, nz, nodes_all), comm),
        out_shape=(
            jax.ShapeDtypeStruct(block, F32),
            jax.ShapeDtypeStruct(block, F32),
            jax.ShapeDtypeStruct((8, 128), F32),
        ),
        in_specs=[anywhere] * 4,
        out_specs=(anywhere, anywhere, pl.BlockSpec(memory_space=pltpu.VMEM)),
        scratch_shapes=scratch,
        compiler_params=pltpu.CompilerParams(
            collective_id=0 if comm else None, has_side_effects=True, vmem_limit_bytes=60 * 1024 * 1024),
    )(positions, velocities, link_codes, fixed_nodes)
    tiles = (2, deep, rows // 8, 8, cols)
    velocity = factor * kicked.reshape(tiles)
    position = position.reshape(tiles) + TIME_STEP * velocity
    return (position.reshape(block), velocity.reshape(block))


def solution(mesh, comm=True):
    sizes = tuple(mesh.shape[a] for a in AXES)
    in_specs = (
        P(None, "gz", "gy", "gx"),
        P(None, "gz", "gy", "gx"),
        P("gz", "gy", "gx"),
        P("gz", "gy", "gx"),
    )
    out_specs = (P(None, "gz", "gy", "gx"), P(None, "gz", "gy", "gx"))
    return jax.shard_map(
        functools.partial(local, sizes, comm), mesh=mesh, in_specs=in_specs, out_specs=out_specs, check_vma=False)
```

time: 407 us -> 66.6 us (0.16)
  blocking collectives: 297 us -> 0 us
  Pallas kernels: 0 us -> 62.4 us
  starting transfers between devices: 52.2 us -> 0 us
  other arithmetic: 37.3 us -> 2.68 us
  local copies, waits for them, and re-layouts: 11.7 us -> 0.67 us
  between operations: 5.42 us -> 0.65 us
    psum x3 -> x0, blocking collectives: 297 us -> none  [total_energy(): return lax.psum(0.5 * jnp.sum(kicked * kicked), ('gx', 'gy', 'gz'))]
    pallas_call x0 -> x1, Pallas kernels: none -> 62.4 us  [local(): pl.pallas_call(functools.partial(kernel, (nx, ny, nz, nodes_all), comm),...]
    ppermute x18 -> x0, starting transfers between devices: 52.2 us -> none  [the longest x9 31.9 us: extended(): lax.ppermute(lax.slice_in_dim(block, block.shape[dim] - width, None, axis...]
    another operation x6 -> x0, other arithmetic: 27.8 us -> none  [spring_force(): return jnp.stack([force_y, force_x])]
    slice x16 -> x0, local copies, waits for them, and re-layouts: 8.05 us -> none  [the longest x11 7.48 us: extended(): lax.slice_in_dim(block, block.shape[dim] - width, None, axis=dim)]
    concatenate x6 -> x0, other arithmetic: 4.41 us -> none  [extended(): block = jnp.concatenate([low, block, high], axis=dim)]
  transfers between devices with their start and end apart: 18 -> 0, of which waited for: 3 -> 0; matrix products, arithmetic and copies ran while one was open for 3% -> 0% of each run, Pallas kernels for 0% -> 0%
where the time goes in v1:
time: 66.6 us; the launch traced here: 66.4 us
  Pallas kernels  62.4 us (94%)
  other arithmetic  2.68 us (4%)
  local copies, waits for them, and re-layouts  0.67 us (1%)
    pallas_call x1, Pallas kernels, local(): pl.pallas_call(functools.partial(kernel, (nx, ny, nz, nodes_all), comm),...  62.4 us
    add x1, other arithmetic, local(): position = position.reshape(tiles) + TIME_STEP * velocity  2.68 us

profile of v1, /device:TPU:1, one launch (start us, length us, event | category | flops | bytes accessed | tf_op | source)
XLA Modules:
  0.0 66.4 jit_solution(8690169858858776616)
XLA Ops:
  0.6 62.4 %shard_map.59 = (f32[2,6,128,128]{3,2,1,0:T(8,128)}, f32[2,6,128,128]{3,2,1,0:T(8,128)}, f32[8,128]{1,0:T(8,128)}) custom-call(f32[2,6,128,128]{3,2,1,0:T(8,128)} %refs_0_.1, f32[2,6,128,128]{3,2,1,0:T(8,128)} %refs_1_.1, s32[6,128,128]{2,1,0:T(8,128)} %refs_2_.1, s32[6,128,128]{2,1,0:T(8,128)} %refs_3_.1), custom_call_target="tpu_custom_call" | custom-call | tf_op jit(solution)/shard_map/pallas_call | solution.py:459
  63.0 0.0 copy-start
  63.0 0.7 copy-done
  63.7 2.7 %multiply_add_fusion = (f32[2,6,128,128]{3,2,1,0:T(8,128)}, f32[2,6,128,128]{3,2,1,0:T(8,128)}) fusion(f32[2,6,128,128]{3,2,1,0:T(8,128)} %get-tuple-element.5, f32[2,6,128,128]{3,2,1,0:T(8,128)} %get-tuple-element.7, f32[128,128]{1,0:T(8,128)S(1)} %broadcast_bitcast_fusion), kind=kLoop, calls=%fused_computation | loop fusion | flops 589824 | bytes 3211264 | tf_op jit(solution)/shard_map/add | solution.py:474
  (1 shorter events, 0.0 us)
Async XLA Ops:
  63.0 0.7 %copy-start = (f32[8,128]{1,0:T(8,128)S(1)}, f32[8,128]{1,0:T(8,128)}, u32[]{:S(2)}) copy-start(f32[8,128]{1,0:T(8,128)} %get-tuple-element.6) | copy-start | bytes 12292

commit v2 on v1

--- a/solution.py
+++ b/solution.py
@@ -55,7 +55,7 @@
      pos, rolled, kick, force, below, below_right, codes, fixed, m_plane, m_one, m_two, mov,
      z_in, edge_own, edge_in, row_own, row_in, edge_pos, edge_halo, row_pos, up_pos, down_pos,
      m_edge, m_top, edge_force, sum_src, sum_a, sum_b,
-     load_sem, out_sem, halo_send, halo_recv, sum_send, sum_recv) = refs
+     load_sem, out_sem, halo_send, halo_recv, sum_send, sum_recv, greeted) = refs
     nx, ny, nz, nodes_all = sizes
     chips = ny // 2
     me = {a: lax.axis_index(a) for a in AXES}
@@ -86,10 +86,25 @@
 
     if comm:
         barrier = pltpu.get_barrier_semaphore()
-        near = [shifted(0, 1, 0), shifted(0, -1, 0)] + [shifted(i, j, 0) for i in (1, -1) for j in (1, -1)]
-        peers = near + [by_chip(*o) for o in group_a + group_b]
+        beside = [(1, 0, 0, 0), (nx - 1, 0, 0, 0), (0, 0, 0, 1), (0, 0, 0, nz - 1),
+                  (0, 1, 0, 0), (0, chips - 1, 0, 0), (0, 0, 1, 0)]
+        peers = [shifted(i, j, 0) for i in (1, -1, 0) for j in (1, -1)] + [by_chip(*o) for o in beside]
         for peer in peers:
             pl.semaphore_signal(barrier, inc=1, device_id=peer, device_id_type=MESH)
+    rounds = [
+        [(1, 0, 0, 0), (nx - 1, 0, 0, 0), (0, 0, 0, 1), (0, 0, 0, nz - 1), (0, 1, 0, 0), (0, chips - 1, 0, 0), (0, 0, 1, 0)],
+        [(2 % nx, 0, 0, 0), (nx - 2, 0, 0, 0), (0, 0, 0, 2 % nz), (0, 0, 0, nz - 2)],
+        [(0, 0, 1, 0), (0, 1, 0, 0), (0, 2 % chips, 0, 0), (0, chips - 1, 0, 0)],
+    ]
+
+    def greet(n):
+        if comm:
+            for o in rounds[n]:
+                pl.semaphore_signal(greeted.at[n], inc=1, device_id=by_chip(*o), device_id_type=MESH)
+
+    def meet(n):
+        if comm:
+            pl.semaphore_wait(greeted.at[n], len(rounds[n]))
 
     lane = lax.broadcasted_iota(jnp.int32, (8, 128), 1)
     is_last = lane == 127
@@ -145,9 +160,10 @@
         pltpu.make_async_remote_copy(
             src_ref=got, dst_ref=got, send_sem=sum_send.at[it, phase], recv_sem=sum_recv.at[it, phase],
             device_id=by_chip(*group[0]), device_id_type=MESH).wait_recv()
-        for k in range(1, len(group) + 1):
-            value = value + buffer[it, k]
-        return value
+        terms = [value] + [buffer[it, k] for k in range(1, len(group) + 1)]
+        while len(terms) > 1:
+            terms = [a + b for a, b in zip(terms[::2], terms[1::2])] + (terms[-1:] if len(terms) % 2 else [])
+        return terms[0]
 
     def wait_sums_sent(it):
         for phase, (group, buffer) in enumerate(((group_a, sum_a), (group_b, sum_b))):
@@ -158,6 +174,12 @@
 
     row_own[...] = jnp.zeros_like(row_own)
     loads[0].wait()
+    if comm:
+        pl.semaphore_wait(barrier, len(peers))
+        copies = [halo_copies(0, pos)]
+        for c in copies[0][:2]:
+            c.start()
+    greet(0)
     pack_rows(0, pos)
 
     def pack_positions(g, packed):
@@ -175,10 +197,10 @@
             edge_own[0, c, 8 * j:8 * j + 8, :] = packed[2 * c + j]
 
     if comm:
-        pl.semaphore_wait(barrier, len(peers))
-        copies = [halo_copies(0, pos)]
-        for c in copies[0]:
+        for c in copies[0][2:]:
             c.start()
+    meet(0)
+    greet(1)
 
     loads[1].wait()
     loads[3].wait()
@@ -251,6 +273,9 @@
 
         lax.fori_loop(0, 6, advance, 0, unroll=6)
 
+        if first:
+            meet(1)
+            greet(2)
         if comm:
             for n in range(2, 10):
                 copies[it][n].wait_recv()
@@ -325,6 +350,8 @@
 
         lax.fori_loop(0, 6, in_plane, 0)
 
+        if first:
+            meet(2)
         if comm:
             for n in range(2):
                 copies[it][n].wait()
@@ -454,21 +481,22 @@
         pltpu.SemaphoreType.DMA((ITERS, 10)),
         pltpu.SemaphoreType.DMA((ITERS, 2)),
         pltpu.SemaphoreType.DMA((ITERS, 2)),
+        pltpu.SemaphoreType.REGULAR((3,)),
     ]
     anywhere = pl.BlockSpec(memory_space=pltpu.MemorySpace.HBM)
     position, kicked, factor = pl.pallas_call(
         functools.partial(kernel, (nx, ny, nz, nodes_all), comm),
         out_shape=(
-            jax.ShapeDtypeStruct(block, F32),
-            jax.ShapeDtypeStruct(block, F32),
-            jax.ShapeDtypeStruct((8, 128), F32),
+            pltpu.VMEM(block, F32),
+            pltpu.VMEM(block, F32),
+            pltpu.VMEM((8, 128), F32),
         ),
         in_specs=[anywhere] * 4,
-        out_specs=(anywhere, anywhere, pl.BlockSpec(memory_space=pltpu.VMEM)),
+        out_specs=(pl.BlockSpec(memory_space=pltpu.VMEM),) * 3,
         scratch_shapes=scratch,
         compiler_params=pltpu.CompilerParams(
-            collective_id=0 if comm else None, has_side_effects=True, vmem_limit_bytes=60 * 1024 * 1024),
-    )(positions, velocities, link_codes, fixed_nodes)
+            collective_id=0 if comm else None, has_side_effects=True, vmem_limit_bytes=32 * 1024 * 1024),
+    )(*(pltpu.with_memory_space_constraint(a, pltpu.HBM) for a in (positions, velocities, link_codes, fixed_nodes)))
     tiles = (2, deep, rows // 8, 8, cols)
     velocity = factor * kicked.reshape(tiles)
     position = position.reshape(tiles) + TIME_STEP * velocity

time: 66.6 us -> 61.2 us (0.919)
  Pallas kernels: 62.4 us -> 59.1 us
  other arithmetic: 2.68 us -> 1.32 us
    pallas_call x1, Pallas kernels: 62.4 us -> 59.1 us  [local(): pl.pallas_call(functools.partial(kernel, (nx, ny, nz, nodes_all), comm),...]
    add x1, other arithmetic: 2.68 us -> 1.32 us  [local(): position = position.reshape(tiles) + TIME_STEP * velocity]
where the time goes in v2:
time: 61.2 us; the launch traced here: 61.1 us
  Pallas kernels  59.1 us (97%)
  other arithmetic  1.32 us (2%)
  between operations  0.65 us (1%)
    pallas_call x1, Pallas kernels, local(): pl.pallas_call(functools.partial(kernel, (nx, ny, nz, nodes_all), comm),...  59.1 us
    add x1, other arithmetic, local(): position = position.reshape(tiles) + TIME_STEP * velocity  1.32 us

profile of v2, /device:TPU:1, one launch (start us, length us, event | category | flops | bytes accessed | tf_op | source)
XLA Modules:
  0.0 61.1 jit_solution(16465991174662309160)
XLA Ops:
  0.6 59.1 %shard_map.59 = (f32[2,6,128,128]{3,2,1,0:T(8,128)S(1)}, f32[2,6,128,128]{3,2,1,0:T(8,128)S(1)}, f32[8,128]{1,0:T(8,128)S(1)}) custom-call(f32[2,6,128,128]{3,2,1,0:T(8,128)} %refs_0_.1, f32[2,6,128,128]{3,2,1,0:T(8,128)} %refs_1_.1, s32[6,128,128]{2,1,0:T(8,128)} %refs_2_.1, s32[6,128,128]{2,1,0:T(8,128)} %refs_3_.1), custom_call_target="tpu_custom_call" | custom-call | tf_op jit(solution)/shard_map/pallas_call | solution.py:487
  59.8 1.3 %multiply_add_fusion = (f32[2,6,128,128]{3,2,1,0:T(8,128)}, f32[2,6,128,128]{3,2,1,0:T(8,128)}) fusion(f32[2,6,128,128]{3,2,1,0:T(8,128)S(1)} %get-tuple-element.5, f32[2,6,128,128]{3,2,1,0:T(8,128)S(1)} %get-tuple-element.7, f32[128,128]{1,0:T(8,128)S(1)} %broadcast_bitcast_fusion), kind=kLoop, calls=%fused_computation | loop fusion | flops 589824 | bytes 3211264 | tf_op jit(solution)/shard_map/add | solution.py:502
  (1 shorter events, 0.0 us)

commit v3 on v2

--- a/solution.py
+++ b/solution.py
@@ -54,7 +54,7 @@
     (pos_in, vel_in, code_in, fix_in, pos_out, kick_out, fac_out,
      pos, rolled, kick, force, below, below_right, codes, fixed, m_plane, m_one, m_two, mov,
      z_in, edge_own, edge_in, row_own, row_in, edge_pos, edge_halo, row_pos, up_pos, down_pos,
-     m_edge, m_top, edge_force, sum_src, sum_a, sum_b,
+     m_edge, m_top, edge_force, edge_next, sum_src, sum_a, sum_b,
      load_sem, out_sem, halo_send, halo_recv, sum_send, sum_recv, greeted) = refs
     nx, ny, nz, nodes_all = sizes
     chips = ny // 2
@@ -72,8 +72,8 @@
         ox, chip, core, oz = o
         return -(min(ox, nx - ox) + min(chip, chips - chip) + min(oz, nz - oz)) - 0.1 * core
 
-    group_a = sorted([(i, 0, c, 0) for i in range(nx) for c in range(2) if i or c], key=far)
-    group_b = sorted([(0, c, 0, k) for c in range(chips) for k in range(nz) if c or k], key=far)
+    group_a = sorted([(0, c, k, 0) for c in range(chips) for k in range(2) if c or k], key=far)
+    group_b = sorted([(i, 0, 0, k) for i in range(nx) for k in range(nz) if i or k], key=far)
 
     loads = [
         pltpu.make_async_copy(pos_in, pos.at[:, :, pl.ds(0, 128), :], load_sem.at[0]),
@@ -93,8 +93,8 @@
             pl.semaphore_signal(barrier, inc=1, device_id=peer, device_id_type=MESH)
     rounds = [
         [(1, 0, 0, 0), (nx - 1, 0, 0, 0), (0, 0, 0, 1), (0, 0, 0, nz - 1), (0, 1, 0, 0), (0, chips - 1, 0, 0), (0, 0, 1, 0)],
-        [(2 % nx, 0, 0, 0), (nx - 2, 0, 0, 0), (0, 0, 0, 2 % nz), (0, 0, 0, nz - 2)],
-        [(0, 0, 1, 0), (0, 1, 0, 0), (0, 2 % chips, 0, 0), (0, chips - 1, 0, 0)],
+        [(2, 0, 0, 0), (nx - 2, 0, 0, 0), (0, 0, 0, 2), (0, 0, 0, nz - 2), (0, 0, 1, 0)],
+        [(0, 0, 0, k) for k in range(1, nz)],
     ]
 
     def greet(n):
@@ -276,14 +276,14 @@
         if first:
             meet(1)
             greet(2)
-        if comm:
+        if comm and first:
             for n in range(2, 10):
                 copies[it][n].wait_recv()
 
         for c in range(2):
             own, up, down = row_own[it, 0, c], row_in[it, 0, c], row_in[it, 1, c]
             edges = edge_own[it, c]
-            halo = build_halo(it, c)
+            halo = build_halo(it, c) if first else [edge_next[c, 8 * n:8 * n + 8, :] for n in range(4)]
             if not first:
                 own = row_pos[c] + scale * own
                 up = up_pos[c] + scale * up
@@ -348,7 +348,7 @@
                     force[c, z, rows, :] = here + lanes_right(right)
             return carry
 
-        lax.fori_loop(0, 6, in_plane, 0)
+        lax.fori_loop(0, 6, in_plane, 0, unroll=2)
 
         if first:
             meet(2)
@@ -401,19 +401,21 @@
 
         energy, *packed = lax.fori_loop(0, 8, depth, (zero,) * 5, unroll=4)
 
+        total = jnp.sum(energy, axis=0, keepdims=True)
+        send_sum(it, 0, group_a, sum_a, total)
         if it < ITERS - 1:
+            if comm:
+                copies.append(halo_copies(it + 1, kick))
+                for c in copies[it + 1][:2]:
+                    c.start()
             pack_rows(it + 1, kick)
             for c in range(2):
                 for j in range(2):
                     edge_own[it + 1, c, 8 * j:8 * j + 8, :] = packed[2 * c + j]
-
-        total = jnp.sum(energy, axis=0, keepdims=True)
-        send_sum(it, 0, group_a, sum_a, total)
-        if comm and it < ITERS - 1:
-            copies.append(halo_copies(it + 1, kick))
-            for c in copies[it + 1]:
-                c.start()
-        if it == ITERS - 1:
+            if comm:
+                for c in copies[it + 1][2:]:
+                    c.start()
+        else:
             outs = [
                 pltpu.make_async_copy(pos.at[:, :, pl.ds(0, 128), :], pos_out, out_sem.at[0]),
                 pltpu.make_async_copy(kick, kick_out, out_sem.at[1]),
@@ -422,6 +424,16 @@
                 c.start()
         total = take_sum(it, 0, group_a, sum_a, total)
         send_sum(it, 1, group_b, sum_b, total)
+        if it < ITERS - 1:
+            if comm:
+                for n in range(2, 10):
+                    copies[it + 1][n].wait_recv()
+            for c in range(2):
+                for n, h in enumerate(build_halo(it + 1, c)):
+                    edge_next[c, 8 * n:8 * n + 8, :] = h
+        else:
+            for c in outs:
+                c.wait()
         total = take_sum(it, 1, group_b, sum_b, total)
         kinetic = 0.5 * jnp.sum(total, axis=1, keepdims=True)
         factor = jnp.minimum(1.0, jnp.sqrt(ENERGY_CAP * nodes_all / (kinetic + EPSILON)))
@@ -430,8 +442,6 @@
         damp = DAMPING * factor
 
     fac_out[...] = factor
-    for c in outs:
-        c.wait()
     if comm:
         for it in range(ITERS):
             for c in copies[it][2:]:
@@ -472,9 +482,10 @@
         vmem((3, 16, 128), F32),
         vmem((3, 8, 128), F32),
         vmem((2, 16, 128), F32),
+        vmem((2, 32, 128), F32),
         vmem((ITERS, 2, 1, 128), F32),
-        vmem((ITERS, 2 * nx, 1, 128), F32),
-        vmem((ITERS, ny // 2 * nz, 1, 128), F32),
+        vmem((ITERS, ny, 1, 128), F32),
+        vmem((ITERS, nx * nz, 1, 128), F32),
         pltpu.SemaphoreType.DMA((4,)),
         pltpu.SemaphoreType.DMA((2,)),
         pltpu.SemaphoreType.DMA((ITERS, 10)),

time: 61.2 us -> 59.9 us (0.979)
  Pallas kernels: 59.1 us -> 57.8 us
    pallas_call x1, Pallas kernels: 59.1 us -> 57.8 us  [local(): pl.pallas_call(functools.partial(kernel, (nx, ny, nz, nodes_all), comm),...]
where the time goes in v3:
time: 59.9 us; the launch traced here: 59.8 us
  Pallas kernels  57.8 us (96%)
  other arithmetic  1.32 us (2%)
  between operations  0.65 us (1%)
    pallas_call x1, Pallas kernels, local(): pl.pallas_call(functools.partial(kernel, (nx, ny, nz, nodes_all), comm),...  57.8 us
    add x1, other arithmetic, local(): position = position.reshape(tiles) + TIME_STEP * velocity  1.32 us

profile of v3, /device:TPU:1, one launch (start us, length us, event | category | flops | bytes accessed | tf_op | source)
XLA Modules:
  0.0 59.8 jit_solution(2377690024696011851)
XLA Ops:
  0.6 57.8 %shard_map.59 = (f32[2,6,128,128]{3,2,1,0:T(8,128)S(1)}, f32[2,6,128,128]{3,2,1,0:T(8,128)S(1)}, f32[8,128]{1,0:T(8,128)S(1)}) custom-call(f32[2,6,128,128]{3,2,1,0:T(8,128)} %refs_0_.1, f32[2,6,128,128]{3,2,1,0:T(8,128)} %refs_1_.1, s32[6,128,128]{2,1,0:T(8,128)} %refs_2_.1, s32[6,128,128]{2,1,0:T(8,128)} %refs_3_.1), custom_call_target="tpu_custom_call" | custom-call | tf_op jit(solution)/shard_map/pallas_call | solution.py:498
  58.5 1.3 %multiply_add_fusion = (f32[2,6,128,128]{3,2,1,0:T(8,128)}, f32[2,6,128,128]{3,2,1,0:T(8,128)}) fusion(f32[2,6,128,128]{3,2,1,0:T(8,128)S(1)} %get-tuple-element.5, f32[2,6,128,128]{3,2,1,0:T(8,128)S(1)} %get-tuple-element.7, f32[128,128]{1,0:T(8,128)S(1)} %broadcast_bitcast_fusion), kind=kLoop, calls=%fused_computation | loop fusion | flops 589824 | bytes 3211264 | tf_op jit(solution)/shard_map/add | solution.py:513
  (1 shorter events, 0.0 us)

commit v4 on v3

--- a/solution.py
+++ b/solution.py
@@ -135,7 +135,8 @@
         for side, (oy, which) in enumerate(((1, 1), (-1, 0))):
             out.append((row_own.at[it, which], row_in.at[it, side], shifted(0, oy, 0)))
         for slot, (ox, oy) in enumerate(COLUMN_PEERS):
-            out.append((edge_own.at[it], edge_in.at[it, slot], shifted(ox, oy, 0)))
+            part = pl.ds(0, 16) if oy == 0 else pl.ds(8 if oy == 1 else 0, 8)
+            out.append((edge_own.at[it, :, part, :], edge_in.at[it, slot, :, part, :], shifted(ox, oy, 0)))
         return [
             pltpu.make_async_remote_copy(
                 src_ref=s, dst_ref=d, send_sem=halo_send.at[it, n], recv_sem=halo_recv.at[it, n],
@@ -231,7 +232,7 @@
             out[j] = out[j] + gather_edges(kept, g)
         return tuple(out)
 
-    edge_codes = lax.fori_loop(0, 8, masks, (jnp.zeros((8, 128), jnp.int32),) * 2, unroll=2)
+    edge_codes = lax.fori_loop(0, 8, masks, (jnp.zeros((8, 128), jnp.int32),) * 2, unroll=4)
     for j in range(2):
         for n, (first, last) in enumerate(((5, 7), (1, 0), (6, 4))):
             m_edge[n, 8 * j:8 * j + 8, :] = jnp.where(odd8, bit(edge_codes[j], first, plane), bit(edge_codes[j], last, plane))

time: 59.9 us -> 59.9 us (level)
  no operation moved by 1% of the time
where the time goes in v4:
time: 59.9 us; the launch traced here: 59.8 us
  Pallas kernels  57.8 us (96%)
  other arithmetic  1.32 us (2%)
  between operations  0.65 us (1%)
    pallas_call x1, Pallas kernels, local(): pl.pallas_call(functools.partial(kernel, (nx, ny, nz, nodes_all), comm),...  57.8 us
    add x1, other arithmetic, local(): position = position.reshape(tiles) + TIME_STEP * velocity  1.32 us

profile of v4, /device:TPU:1, one launch (start us, length us, event | category | flops | bytes accessed | tf_op | source)
XLA Modules:
  0.0 59.8 jit_solution(7494841195644871951)
XLA Ops:
  0.6 57.8 %shard_map.59 = (f32[2,6,128,128]{3,2,1,0:T(8,128)S(1)}, f32[2,6,128,128]{3,2,1,0:T(8,128)S(1)}, f32[8,128]{1,0:T(8,128)S(1)}) custom-call(f32[2,6,128,128]{3,2,1,0:T(8,128)} %refs_0_.1, f32[2,6,128,128]{3,2,1,0:T(8,128)} %refs_1_.1, s32[6,128,128]{2,1,0:T(8,128)} %refs_2_.1, s32[6,128,128]{2,1,0:T(8,128)} %refs_3_.1), custom_call_target="tpu_custom_call" | custom-call | tf_op jit(solution)/shard_map/pallas_call | solution.py:499
  58.5 1.3 %multiply_add_fusion = (f32[2,6,128,128]{3,2,1,0:T(8,128)}, f32[2,6,128,128]{3,2,1,0:T(8,128)}) fusion(f32[2,6,128,128]{3,2,1,0:T(8,128)S(1)} %get-tuple-element.5, f32[2,6,128,128]{3,2,1,0:T(8,128)S(1)} %get-tuple-element.7, f32[128,128]{1,0:T(8,128)S(1)} %broadcast_bitcast_fusion), kind=kLoop, calls=%fused_computation | loop fusion | flops 589824 | bytes 3211264 | tf_op jit(solution)/shard_map/add | solution.py:514
  (1 shorter events, 0.0 us)
